TPU v7x, 512 devices: a whole 4x8x8 slice. The times are simulated.
512 devices in a mesh: row: 8 (over z), col: 16 (over y, core), layer: 4 (over x).
Axes of the slice: x: 4, y: 8, z: 8, core: 2. Of those that a mesh axis runs over, the one named last changes fastest.
Arguments:
- panel_values: bfloat16 [16384, 8192], P('row', ('layer', 'col')), may hold values from -6 to 6
- slab_values: bfloat16 [8192, 6144], P(('layer', 'row'), 'col'), may hold values from -0.09375 to 0.09375
- pattern_panel: int32 [128, 64], P('row', ('layer', 'col')), may hold values from 0 to 1, as said below
- pattern_result: int32 [128, 48], P(('row', 'layer'), 'col'), may hold values 0 or 1
Outputs:
- product_slab: bfloat16 [16384, 6144], P(('row', 'layer'), 'col')
Inputs may be any that keep to these rules, and one draw needn't show every extreme that they name: `pattern_panel`: in every group of 16 blocks that one device holds of one block column (block rows r * 16 to r * 16 + 15), 1 to 8 are 1; some group reaches this bound: every group of block column 0 has exactly 8.
All inputs are finite; a program needn't handle non-finite values. No bound on the sum of `pattern_result` on one device may be relied on, other than what follows from the above.
Results may differ from a plain program's by a relative error of at most 0.001.
Values may be sent and summed in bfloat16 or wider, within the bound.
A program may use at most 64 MiB of HBM per device.

v0:
```python
import jax
import jax.numpy as jnp
from jax import lax
from jax.sharding import PartitionSpec as P


def per_device(panel_values, slab_values, pattern_panel, pattern_result):
    block = panel_values.shape[1]
    row_blocks = pattern_panel.shape[0]
    gathered = lax.all_gather(slab_values, "row", axis=0, tiled=True)
    flags = pattern_panel[:, 0]
    blocks_here = panel_values.reshape(row_blocks, block, block)
    masked = (blocks_here * flags.astype(jnp.bfloat16)[:, None, None]).reshape(
        row_blocks * block, block
    )
    partial_value = jnp.dot(
        lax.all_gather(masked, "col", axis=1, tiled=True),
        gathered,
        preferred_element_type=jnp.float32,
    )
    shares = lax.psum_scatter(partial_value, "layer", scatter_dimension=0, tiled=True)
    out_blocks = pattern_result.shape[0]
    col_blocks = pattern_result.shape[1]
    keeper = pattern_result.astype(jnp.float32)
    filtered = shares.reshape(out_blocks, block, col_blocks, block) * keeper[:, None, :, None]
    return filtered.reshape(shares.shape).astype(jnp.bfloat16)


def solution(mesh):
    placed = (
        P("row", ("layer", "col")),
        P(("layer", "row"), "col"),
        P("row", ("layer", "col")),
        P(("row", "layer"), "col"),
    )
    return jax.shard_map(
        per_device,
        mesh=mesh,
        in_specs=placed,
        out_specs=P(("row", "layer"), "col"),
        check_vma=False,
    )
```

profile of v0, /device:TPU:1, one launch (start us, length us, event | category | flops | bytes accessed | tf_op | source)
XLA Modules:
  0.0 186.3 jit_solution(16902584694863488766)
XLA Ops:
  6.5 0.0 all-gather.5.cloned.1.call-start
  6.5 0.7 all-gather.5.cloned.1.call-update
  7.3 0.0 all-gather.3.cloned.1.call-start
  7.3 0.7 convert_bitcast_fusion
  8.0 0.1 broadcast_bitcast_fusion
  8.0 2.2 %broadcast_multiply_fusion = bf16[2048,128]{1,0:T(8,128)(2,1)} fusion(bf16[2048,128]{1,0:T(8,128)(2,1)} %param.4, bf16[2048]{0:T(1024)(128)(2,1)S(1)} %broadcast_bitcast_fusion), kind=kLoop, calls=%fused_computation.2 | loop fusion | flops 262144 | bytes 1052672 | tf_op jit(solution)/shard_map/mul | solution.py:13
  10.3 0.0 all-gather.3.cloned.1.call-update
  10.3 0.0 reduce-scatter.2.cloned.1.call-start
  10.3 44.2 %all-gather.5.cloned.1.call-done = bf16[2048,384]{1,0:T(8,128)(2,1)} async-done(((bf16[256,384]{1,0:T(8,128)(2,1)}), bf16[2048,384]{1,0:T(8,128)(2,1)}) %all-gather.5.cloned.1.call-update) | async-done | bytes 1572880 | tf_op jit(solution)/shard_map/all_gather | solution.py:10
  54.5 73.2 %all-gather.3.cloned.1.call-done = bf16[2048,2048]{1,0:T(8,128)(2,1)} async-done(((bf16[2048,128]{1,0:T(8,128)(2,1)}), bf16[2048,2048]{1,0:T(8,128)(2,1)}) %all-gather.3.cloned.1.call-update) | async-done | bytes 8388624 | tf_op jit(solution)/shard_map/all_gather | solution.py:17
  127.7 10.1 %fusion = f32[2048,384]{1,0:T(8,128)} fusion(bf16[2048,2048]{1,0:T(8,128)(2,1)} %all-gather.3.cloned.1.call-done, bf16[2048,384]{1,0:T(8,128)(2,1)} %all-gather.5.cloned.1.call-done), kind=kOutput, calls=%fused_computation.5 | convolution fusion | flops 3221225472 | bytes 13107200 | tf_op jit(solution)/shard_map/dot_general | solution.py:16
  137.8 0.0 copy-start
  137.8 0.0 reduce-scatter.2.cloned.1.call-update
  137.8 0.7 copy-done
  138.4 0.1 copy.5
  138.5 0.2 mul.28
  138.7 0.1 copy.9
  138.8 0.3 copy.6
  139.1 38.8 %reduce-scatter.2.cloned.1.call-done = f32[512,384]{1,0:T(8,128)} async-done(((f32[2048,384]{1,0:T(8,128)}), f32[512,384]{1,0:T(8,128)}) %reduce-scatter.2.cloned.1.call-update) | async-done | bytes 786448 | tf_op jit(solution)/shard_map/reduce_scatter | solution.py:21
  177.8 2.0 %multiply_convert_fusion = bf16[512,384]{1,0:T(8,128)(2,1)} fusion(f32[512,384]{1,0:T(8,128)} %reduce-scatter.2.cloned.1.call-done, f32[512,384]{1,0:T(8,128)S(1)} %copy.6), kind=kLoop, calls=%fused_computation.1 | loop fusion | flops 393216 | bytes 1966080 | tf_op jit(solution)/shard_map/convert_element_type | solution.py:26
  (1 shorter events, 0.0 us)
Async XLA Ops:
  6.5 48.0 %all-gather.5.cloned.1.call-start = ((), (), s32[]{:S(2)}) async-start(), calls=%async_computation.2 | async-start | bytes 1769472 | tf_op jit(solution)/shard_map/all_gather | solution.py:10
  7.3 120.5 %all-gather.3.cloned.1.call-start = ((), (), s32[]{:S(2)}) async-start(), calls=%async_computation.1 | async-start | bytes 8912896 | tf_op jit(solution)/shard_map/all_gather | solution.py:17
  10.3 167.5 %reduce-scatter.2.cloned.1.call-start = ((), (), s32[]{:S(2)}) async-start(), calls=%async_computation.3 | async-start | bytes 3932160 | tf_op jit(solution)/shard_map/reduce_scatter | solution.py:21
  137.8 0.7 copy-start
Sparse Core Ops, SparseCore 0:
  9.4 45.0 all-gather.4
  56.6 71.0 all-gather.2
  137.9 39.8 reduce-scatter.1
where the time goes:
time: 187 us; the launch traced here: 186 us
  waiting for transfers between devices  157 us (84%)
  between operations  13.1 us (7%)
  matrix products  10.1 us (5%)
  other arithmetic  4.83 us (3%)
    all_gather x1, waiting for transfers between devices, per_device(): lax.all_gather(masked, 'col', axis=1, tiled=True)  73.2 us
    all_gather x1, waiting for transfers between devices, per_device(): gathered = lax.all_gather(slab_values, 'row', axis=0, tiled=True)  44.2 us
    reduce_scatter x1, waiting for transfers between devices, per_device(): lax.psum_scatter(partial_value, 'layer', scatter_dimension=0, tiled=True)  38.8 us
    dot_general x1, matrix products, per_device(): jnp.dot(lax.all_gather(masked, 'col', axis=1, tiled=True), gathered, pref...  10.1 us
  transfers between devices with their start and end apart: 3, of which 3 were waited for; matrix products, arithmetic and copies ran while one was open for 2% of the time, Pallas kernels for 0%

commit v1 on v0

v1 whole, which is shorter than its diff:
```python
import functools

import jax
import jax.numpy as jnp
from jax import lax
from jax.experimental import pallas as pl
from jax.experimental.pallas import tpu as pltpu
from jax.sharding import PartitionSpec as P

BS = 128
RB = 16
NNZ = 8
TAB = 16
NL = 4
UNITS = ((2, 0), (2, 1), (1, 1), (3, 0), (1, 0), (3, 1), (0, 0), (0, 1))
Y_STEP, Z_STEP = 1.31, 1.97


def ring_order(n, pieces, forward):
    order = []
    own = pieces if forward else pieces[::-1]
    for step in range(n // 2):
        order += [(step, q) for q in (own if step < n // 2 - 1 else own[:1])]
    return order


def kernel(n, panel_hbm, slab_hbm, flags, keep, out, *scratch):
    held = scratch[: 2 * n]
    (panel, slab, dense, send_x, mid_x, last_x, own_sem, y_send, y_recv, c_send, c_recv, z_send, z_recv, x_send, x_recv) = scratch[2 * n :]
    col, z, layer = lax.axis_index("col"), lax.axis_index("row"), lax.axis_index("layer")
    y, core = col // 2, lax.rem(col, 2)
    depth = slab_hbm.shape[0]
    part = depth // 2

    panel_in = pltpu.make_async_copy(panel_hbm, panel, own_sem.at[0])
    panel_in.start()
    slab_in = pltpu.make_async_copy(slab_hbm, slab.at[pl.ds(pl.multiple_of(z * depth, depth), depth)], own_sem.at[1])
    slab_in.start()

    def beside(place, count, step):
        return lax.rem(place + step + count, count)

    y_next = {+1: {"col": beside(y, n, 1) * 2 + core}, -1: {"col": beside(y, n, -1) * 2 + core}}
    z_next = {+1: {"row": beside(z, n, 1)}, -1: {"row": beside(z, n, -1)}}
    x_next = {+1: {"layer": beside(layer, NL, 1)}, -1: {"layer": beside(layer, NL, -1)}}
    sibling = {"col": y * 2 + 1 - core}
    neighbours = [y_next[1], y_next[-1], z_next[1], z_next[-1], x_next[1], x_next[-1], sibling]
    barrier = pltpu.get_barrier_semaphore()
    for device in neighbours:
        pl.semaphore_signal(barrier, inc=1, device_id=device, device_id_type=pl.DeviceIdType.MESH)

    rows_of = []
    for ahead, half in UNITS:
        first = lax.rem(layer + ahead, NL) * (RB // NL) + half * 2
        rows_of += [first, first + 1]
    count = jnp.int32(0)
    source = [jnp.int32(0)] * NNZ
    table = jnp.full((TAB, BS), float(NNZ), jnp.float32)
    place_of = lax.broadcasted_iota(jnp.int32, (TAB, BS), 0)
    for p in range(RB):
        flag = flags[rows_of[p]]
        if p > RB - NNZ:
            count = jnp.maximum(count, p - (RB - NNZ))
        for s in range(max(0, p - (RB - NNZ)), min(p, NNZ - 1) + 1):
            source[s] = jnp.where((flag == 1) & (count == s), rows_of[p], source[s])
        slot = jnp.where(flag == 1, count, NNZ)
        table = jnp.where(place_of == p, slot.astype(jnp.float32), table)
        count = count + flag
    held[0][pl.ds(0, TAB), :] = table.astype(jnp.bfloat16)
    panel_in.wait()
    for s in range(NNZ):
        held[0][pl.ds(TAB + s * BS, BS), :] = panel[source[s]]
    slab_in.wait()
    pl.semaphore_wait(barrier, len(neighbours))

    started = []

    def remote(src, dst, send, recv, device):
        return pltpu.make_async_remote_copy(src_ref=src, dst_ref=dst, send_sem=send, recv_sem=recv, device_id=device, device_id_type=pl.DeviceIdType.MESH)

    def begin(copy):
        copy.start()
        started.append(copy)

    def rows(q):
        return pl.ds(0, TAB + 2 * BS) if q == 0 else pl.ds(TAB + q * 2 * BS, 2 * BS)

    y_order = {d: ring_order(n, [0, 1], d == 1) + ring_order(n, [2, 3], d == 1) for d in (1, -1)}
    z_order = {d: ring_order(n, [0, 1], d == 1) for d in (1, -1)}

    def y_copy(d, i):
        step, q = y_order[d][i]
        src, dst = held[2 * ((-d * step) % n)], held[2 * ((-d * (step + 1)) % n)]
        k = (0 if d == 1 else len(y_order[1])) + i
        return remote(src.at[rows(q)], dst.at[rows(q)], y_send.at[k], y_recv.at[k], y_next[d])

    def c_copy(j, q):
        return remote(held[2 * j].at[rows(q)], held[2 * j + 1].at[rows(q)], c_send.at[4 * j + q], c_recv.at[4 * j + q], sibling)

    def z_copy(d, i, back=0):
        step, q = z_order[d][i]
        k = (0 if d == 1 else len(z_order[1])) + i
        at = slab.at[pl.ds(pl.multiple_of(beside(z, n, -d * (step + back)) * depth + q * part, part), part)]
        return remote(at, at, z_send.at[k], z_recv.at[k], z_next[d])

    def lanes(j, c):
        side = core if c == 0 else 1 - core
        return pl.ds(pl.multiple_of(beside(y, n, j) * 2 * BS + side * BS, BS), BS)

    def unpack(j, c, places):
        ref, where = held[2 * j + c], lanes(j, c)
        slots = range(min(NNZ, places[-1] + 1))
        one_of = {}
        for p in places:
            line = ref[pl.ds(0, TAB), :][p : p + 1, :].astype(jnp.float32)
            for s in slots:
                if p - (RB - NNZ) <= s <= p:
                    one_of[p, s] = (line == float(s)).astype(jnp.bfloat16)

        @pl.loop(0, BS // 16)
        def _(i):
            values = [ref[pl.ds(pl.multiple_of(TAB + s * BS + i * 16, 16), 16), :] for s in slots]
            for p in places:
                terms = [values[s] * one_of[p, s] for s in slots if (p, s) in one_of]
                dense[pl.ds(pl.multiple_of(p * BS + i * 16, 16), 16), where] = functools.reduce(jnp.add, terms)

    def multiply(unit):
        return jnp.dot(dense[pl.ds(unit * 2 * BS, 2 * BS), :], slab[...], preferred_element_type=jnp.float32)

    def x_copy(k, device, dst):
        return remote(send_x.at[k], dst, x_send.at[k], x_recv.at[k], device)

    x_copies = [
        x_copy(0, x_next[1], mid_x.at[0]),
        x_copy(1, x_next[-1], mid_x.at[1]),
        x_copy(2, x_next[1], last_x.at[0]),
        x_copy(3, x_next[-1], last_x.at[1]),
        x_copy(4, x_next[1], last_x.at[2]),
        x_copy(5, x_next[-1], last_x.at[3]),
    ]

    for d in (1, -1):
        for i in range(min(2, len(y_order[d]))):
            if y_order[d][i][0] == 0:
                begin(y_copy(d, i))
        for i in range(min(2, len(z_order[d]))):
            begin(z_copy(d, i))
    for q in range(4):
        begin(c_copy(0, q))

    arrived, passed = {0: {0, 1, 2, 3}}, {0: {0, 1, 2, 3}}
    early, late = list(range(RB // NL)), list(range(RB // NL, RB))
    done = set()
    waited = set()

    def take(j, c, wanted, which):
        if (j, c, which) in done:
            return
        if c == 1:
            for q in wanted:
                if (j, q) not in waited:
                    waited.add((j, q))
                    c_copy(j, q).wait_recv()
        done.add((j, c, which))
        unpack(j, c, early if which == 0 else late)

    def drain(c, source_of):
        for j in range(n):
            have = source_of.get(j, set())
            if {0, 1} <= have:
                take(j, c, (0, 1), 0)
            if {0, 1, 2, 3} <= have:
                take(j, c, (0, 1, 2, 3), 1)

    events = [(Y_STEP * (i + 1), 0, i) for i in range(len(y_order[1]))] + [(Z_STEP * (i + 1), 1, i) for i in range(len(z_order[1]))]
    computed = [0]

    def early_unit(u):
        send_x[u] = multiply(u)
        begin(x_copies[u])

    z_left = len(z_order[1])
    for _, kind, i in sorted(events):
        if kind == 1:
            for d in (1, -1):
                z_copy(d, i, 1).wait_recv()
                if i + 2 < len(z_order[d]):
                    begin(z_copy(d, i + 2))
            z_left -= 1
            continue
        before = {j: set(v) for j, v in passed.items()}
        for d in (1, -1):
            step, q = y_order[d][i]
            j = (-d * (step + 1)) % n
            y_copy(d, i).wait_recv()
            if i + 2 < len(y_order[d]):
                begin(y_copy(d, i + 2))
            begin(c_copy(j, q))
            arrived.setdefault(j, set()).add(q)
            passed.setdefault(j, set()).add(q)
        if i < len(y_order[1]) - 1:
            drain(0, arrived)
            drain(1, before)
            ready = all((j, c, 0) in done for j in range(n) for c in range(2))
            if z_left == 0 and ready and computed[0] < 2:
                early_unit(computed[0])
                computed[0] += 1
    drain(0, arrived)
    drain(1, passed)
    for u in range(computed[0], 2):
        early_unit(u)
    for u in (2, 3):
        early_unit(u)
    for u, k in ((4, 0), (5, 1)):
        own = multiply(u)
        x_copies[k].wait_recv()
        send_x[u] = own + mid_x[k]
        begin(x_copies[u])
    top, low = multiply(6), multiply(7)
    half = 2 * BS

    def finish(total, first):
        for r in range(2):
            for c in range(total.shape[1] // BS):
                kept = keep[first // BS + r, c].astype(jnp.float32)
                out[pl.ds(first + r * BS, BS), pl.ds(c * BS, BS)] = (total[r * BS : (r + 1) * BS, c * BS : (c + 1) * BS] * kept).astype(jnp.bfloat16)

    x_copies[3].wait_recv()
    send_top = top + last_x[1]
    x_copies[2].wait_recv()
    send_low = low + last_x[0]
    x_copies[4].wait_recv()
    finish(send_top + last_x[2], 0)
    x_copies[5].wait_recv()
    finish(send_low + last_x[3], half)
    for copy in started:
        copy.wait_send()


def per_device(n, panel_values, slab_values, pattern_panel, pattern_result):
    block = panel_values.shape[1]
    width = slab_values.shape[1]
    depth = slab_values.shape[0]
    sent_y, sent_z = len(ring_order(n, [0, 1], True)) * 2, len(ring_order(n, [0, 1], True))
    dma = pltpu.SemaphoreType.DMA
    held = [pltpu.VMEM((TAB + NNZ * BS, BS), jnp.bfloat16) for _ in range(2 * n)]
    half = 2 * BS
    return pl.pallas_call(
        functools.partial(kernel, n),
        out_shape=jax.ShapeDtypeStruct((4 * BS, width), jnp.bfloat16),
        in_specs=[
            pl.BlockSpec(memory_space=pl.ANY),
            pl.BlockSpec(memory_space=pl.ANY),
            pl.BlockSpec(memory_space=pltpu.SMEM),
            pl.BlockSpec(memory_space=pltpu.SMEM),
        ],
        out_specs=pl.BlockSpec(memory_space=pltpu.VMEM),
        scratch_shapes=held
        + [
            pltpu.VMEM((RB, BS, BS), jnp.bfloat16),
            pltpu.VMEM((n * depth, width), jnp.bfloat16),
            pltpu.VMEM((RB * BS, n * 2 * BS), jnp.bfloat16),
            pltpu.VMEM((6, half, width), jnp.float32),
            pltpu.VMEM((2, half, width), jnp.float32),
            pltpu.VMEM((4, half, width), jnp.float32),
            dma((2,)),
            dma((2 * sent_y,)),
            dma((2 * sent_y,)),
            dma((4 * n,)),
            dma((4 * n,)),
            dma((2 * sent_z,)),
            dma((2 * sent_z,)),
            dma((6,)),
            dma((6,)),
        ],
        compiler_params=pltpu.CompilerParams(collective_id=0, has_side_effects=True, vmem_limit_bytes=48 * 1024 * 1024),
        cost_estimate=pl.CostEstimate(flops=2 * RB * BS * n * 2 * BS * width, bytes_accessed=1 << 22, transcendentals=0),
    )(panel_values.reshape(RB, BS, block), slab_values, pattern_panel[:, 0], pattern_result)


def solution(mesh):
    placed = (
        P("row", ("layer", "col")),
        P(("layer", "row"), "col"),
        P("row", ("layer", "col")),
        P(("row", "layer"), "col"),
    )
    return jax.shard_map(
        functools.partial(per_device, mesh.shape["row"]),
        mesh=mesh,
        in_specs=placed,
        out_specs=P(("row", "layer"), "col"),
        check_vma=False,
    )
```

time: 187 us -> 71.3 us (0.38)
  waiting for transfers between devices: 157 us -> 0 us
  Pallas kernels: 0 us -> 67.2 us
  between operations: 13.1 us -> 0.01 us
  matrix products: 10.1 us -> 0 us
  other arithmetic: 4.83 us -> 0 us
  local copies, waits for them, and re-layouts: 1.31 us -> 3.4 us
    all_gather x2 -> x0, waiting for transfers between devices: 117 us -> none  [the longest x1 73.2 us: per_device(): lax.all_gather(masked, 'col', axis=1, tiled=True)]
    pallas_call x0 -> x1, Pallas kernels: none -> 67.2 us  [per_device(): pl.pallas_call(functools.partial(kernel, n), out_shape=jax.ShapeDtypeStru...]
    reduce_scatter x1 -> x0, waiting for transfers between devices: 38.8 us -> none  [per_device(): lax.psum_scatter(partial_value, 'layer', scatter_dimension=0, tiled=True)]
    dot_general x1 -> x0, matrix products: 10.1 us -> none  [per_device(): jnp.dot(lax.all_gather(masked, 'col', axis=1, tiled=True), gathered, pref...]
    unnamed x3 -> x9, local copies, waits for them, and re-layouts: 0.71 us -> 3.4 us
    convert_element_type x3 -> x0, other arithmetic: 2.61 us -> none  [the longest x1 1.95 us: per_device(): return filtered.reshape(shares.shape).astype(jnp.bfloat16)]
    mul x1 -> x0, other arithmetic: 2.22 us -> none  [per_device(): blocks_here * flags.astype(jnp.bfloat16)[:, None, None]]
  transfers between devices with their start and end apart: 3 -> 0, of which waited for: 3 -> 0; matrix products, arithmetic and copies ran while one was open for 2% -> 0% of each run, Pallas kernels for 0% -> 0%
where the time goes in v1:
time: 71.3 us; the launch traced here: 70.7 us
  Pallas kernels  67.2 us (94%)
  local copies, waits for them, and re-layouts  3.4 us (5%)
    pallas_call x1, Pallas kernels, per_device(): pl.pallas_call(functools.partial(kernel, n), out_shape=jax.ShapeDtypeStru...  67.2 us
    unnamed x9, local copies, waits for them, and re-layouts  3.4 us

profile of v1, /device:TPU:1, one launch (start us, length us, event | category | flops | bytes accessed | tf_op | source)
XLA Modules:
  0.0 70.7 jit_solution(17830291683464267021)
XLA Ops:
  0.0 0.0 copy-start.2
  0.0 0.0 copy-start.3
  0.0 0.7 copy-done.2
  0.7 0.0 copy-done.3
  0.7 0.0 copy-start
  0.7 1.0 %copy-done = bf16[2048,128]{1,0:T(8,128)(2,1)S(1)} copy-done((bf16[2048,128]{1,0:T(8,128)(2,1)S(1)}, bf16[2048,128]{1,0:T(8,128)(2,1)}, u32[]{:S(2)}) %copy-start) | copy-done | bytes 524312
  1.7 0.0 copy-start.1
  1.7 0.9 %copy-done.1 = bf16[256,384]{1,0:T(8,128)(2,1)S(1)} copy-done((bf16[256,384]{1,0:T(8,128)(2,1)S(1)}, bf16[256,384]{1,0:T(8,128)(2,1)}, u32[]{:S(2)}) %copy-start.1) | copy-done | bytes 196632
  2.7 67.2 %shard_map.46 = bf16[512,384]{1,0:T(8,128)(2,1)S(1)} custom-call(bf16[16,128,128]{2,1,0:T(8,128)(2,1)S(1)} %bitcast.2, bf16[256,384]{1,0:T(8,128)(2,1)S(1)} %copy-done.1, s32[16]{0:T(128)S(1)} %bitcast.3, s32[4,3]{1,0:T(4,128)S(1)} %copy-done.2), custom_call_target="tpu_custom_call" | custom-call | flops 3221225472 | bytes 4194304 | tf_op jit(solution)/shard_map/pallas_call | solution.py:248
  69.9 0.7 %copy.6 = bf16[512,384]{1,0:T(8,128)(2,1)} copy(bf16[512,384]{1,0:T(8,128)(2,1)S(1)} %shard_map.46) | data formatting | bytes 786432
Async XLA Ops:
  0.0 0.7 copy-start.2
  0.0 0.7 copy-start.3
  0.7 1.0 %copy-start = (bf16[2048,128]{1,0:T(8,128)(2,1)S(1)}, bf16[2048,128]{1,0:T(8,128)(2,1)}, u32[]{:S(2)}) copy-start(bf16[2048,128]{1,0:T(8,128)(2,1)} %param.4) | copy-start | bytes 1572868
  1.7 0.9 %copy-start.1 = (bf16[256,384]{1,0:T(8,128)(2,1)S(1)}, bf16[256,384]{1,0:T(8,128)(2,1)}, u32[]{:S(2)}) copy-start(bf16[256,384]{1,0:T(8,128)(2,1)} %slab_hbm.1) | copy-start | bytes 589828

commit v2 on v1

--- a/solution.py
+++ b/solution.py
@@ -13,29 +13,40 @@
 TAB = 16
 NL = 4
 UNITS = ((2, 0), (2, 1), (1, 1), (3, 0), (1, 0), (3, 1), (0, 0), (0, 1))
-Y_STEP, Z_STEP = 1.31, 1.97
-
-
-def ring_order(n, pieces, forward):
-    order = []
-    own = pieces if forward else pieces[::-1]
+Y_STEP, Z_STEP = 1.7, 2.45
+
+
+def ring_order(n, forward, pieces):
+    own = list(range(pieces)) if forward else list(range(pieces))[::-1]
+    return [(step, q) for step in range(n // 2) for q in (own if step < n // 2 - 1 else own[: pieces // 2])]
+
+
+def panel_order(n, forward):
+    a, b, c, d = (0, 1, 2, 3) if forward else (1, 0, 3, 2)
+    last = n // 2 - 1
+    place = {}
     for step in range(n // 2):
-        order += [(step, q) for q in (own if step < n // 2 - 1 else own[:1])]
-    return order
-
-
-def kernel(n, panel_hbm, slab_hbm, flags, keep, out, *scratch):
+        for q, at in ((a, 3 * step), (b, 3 * step + 1), (c, 3 * step + 2 + 3 * (step > 0)), (d, 3 * step + 5.5 + (step > 0) * 1.5)):
+            if step < last or q in (a, c):
+                place[step, q] = at
+    return sorted(place, key=place.get)
+
+
+def triggers(order, depth):
+    after = []
+    for m, (step, q) in enumerate(order):
+        needs = order.index((step - 1, q)) if step else -1
+        after.append(max(after[-1] if after else -1, needs, m - depth))
+    return after
+
+
+def kernel(n, panel_hbm, slab_hbm, flags_hbm, keep_hbm, out, *scratch):
     held = scratch[: 2 * n]
-    (panel, slab, dense, send_x, mid_x, last_x, own_sem, y_send, y_recv, c_send, c_recv, z_send, z_recv, x_send, x_recv) = scratch[2 * n :]
+    (flags, keep, panel, slab, dense, send_x, mid_x, last_x, own_sem, y_send, y_recv, c_send, c_recv, z_send, z_recv, x_send, x_recv) = scratch[2 * n :]
     col, z, layer = lax.axis_index("col"), lax.axis_index("row"), lax.axis_index("layer")
     y, core = col // 2, lax.rem(col, 2)
     depth = slab_hbm.shape[0]
     part = depth // 2
-
-    panel_in = pltpu.make_async_copy(panel_hbm, panel, own_sem.at[0])
-    panel_in.start()
-    slab_in = pltpu.make_async_copy(slab_hbm, slab.at[pl.ds(pl.multiple_of(z * depth, depth), depth)], own_sem.at[1])
-    slab_in.start()
 
     def beside(place, count, step):
         return lax.rem(place + step + count, count)
@@ -49,6 +60,15 @@
     for device in neighbours:
         pl.semaphore_signal(barrier, inc=1, device_id=device, device_id_type=pl.DeviceIdType.MESH)
 
+    flags_in = pltpu.make_async_copy(flags_hbm, flags, own_sem.at[0])
+    flags_in.start()
+    panel_in = pltpu.make_async_copy(panel_hbm, panel, own_sem.at[1])
+    panel_in.start()
+    slab_in = pltpu.make_async_copy(slab_hbm, slab.at[pl.ds(pl.multiple_of(z * depth, depth), depth)], own_sem.at[2])
+    slab_in.start()
+    keep_in = pltpu.make_async_copy(keep_hbm, keep, own_sem.at[3])
+    keep_in.start()
+
     rows_of = []
     for ahead, half in UNITS:
         first = lax.rem(layer + ahead, NL) * (RB // NL) + half * 2
@@ -57,6 +77,7 @@
     source = [jnp.int32(0)] * NNZ
     table = jnp.full((TAB, BS), float(NNZ), jnp.float32)
     place_of = lax.broadcasted_iota(jnp.int32, (TAB, BS), 0)
+    flags_in.wait()
     for p in range(RB):
         flag = flags[rows_of[p]]
         if p > RB - NNZ:
@@ -68,9 +89,15 @@
         count = count + flag
     held[0][pl.ds(0, TAB), :] = table.astype(jnp.bfloat16)
     panel_in.wait()
-    for s in range(NNZ):
-        held[0][pl.ds(TAB + s * BS, BS), :] = panel[source[s]]
+
+    def pack(q):
+        for s in (2 * q, 2 * q + 1):
+            held[0][pl.ds(TAB + s * BS, BS), :] = panel[source[s]]
+
+    pack(0)
+    pack(1)
     slab_in.wait()
+    keep_in.wait()
     pl.semaphore_wait(barrier, len(neighbours))
 
     started = []
@@ -85,8 +112,9 @@
     def rows(q):
         return pl.ds(0, TAB + 2 * BS) if q == 0 else pl.ds(TAB + q * 2 * BS, 2 * BS)
 
-    y_order = {d: ring_order(n, [0, 1], d == 1) + ring_order(n, [2, 3], d == 1) for d in (1, -1)}
-    z_order = {d: ring_order(n, [0, 1], d == 1) for d in (1, -1)}
+    y_order = {d: panel_order(n, d == 1) for d in (1, -1)}
+    z_order = {d: ring_order(n, d == 1, 2) for d in (1, -1)}
+    y_after, z_after = triggers(y_order[1], 4), triggers(z_order[1], 2)
 
     def y_copy(d, i):
         step, q = y_order[d][i]
@@ -139,12 +167,20 @@
         x_copy(5, x_next[-1], last_x.at[3]),
     ]
 
-    for d in (1, -1):
-        for i in range(min(2, len(y_order[d]))):
-            if y_order[d][i][0] == 0:
-                begin(y_copy(d, i))
-        for i in range(min(2, len(z_order[d]))):
-            begin(z_copy(d, i))
+    def follow(copy_of, after, event):
+        for i, at in enumerate(after):
+            if at == event:
+                for d in (1, -1):
+                    begin(copy_of(d, i))
+
+    first, rest = [(d, i) for i, at in enumerate(y_after) if at == -1 for d in (1, -1)], (2, 3)
+    for d, i in first[:4] if n > 2 else ():
+        begin(y_copy(d, i))
+    follow(z_copy, z_after, -1)
+    for q in rest:
+        pack(q)
+    for d, i in first[4:] if n > 2 else first:
+        begin(y_copy(d, i))
     for q in range(4):
         begin(c_copy(0, q))
 
@@ -184,8 +220,7 @@
         if kind == 1:
             for d in (1, -1):
                 z_copy(d, i, 1).wait_recv()
-                if i + 2 < len(z_order[d]):
-                    begin(z_copy(d, i + 2))
+            follow(z_copy, z_after, i)
             z_left -= 1
             continue
         before = {j: set(v) for j, v in passed.items()}
@@ -193,11 +228,10 @@
             step, q = y_order[d][i]
             j = (-d * (step + 1)) % n
             y_copy(d, i).wait_recv()
-            if i + 2 < len(y_order[d]):
-                begin(y_copy(d, i + 2))
             begin(c_copy(j, q))
             arrived.setdefault(j, set()).add(q)
             passed.setdefault(j, set()).add(q)
+        follow(y_copy, y_after, i)
         if i < len(y_order[1]) - 1:
             drain(0, arrived)
             drain(1, before)
@@ -241,29 +275,26 @@
     block = panel_values.shape[1]
     width = slab_values.shape[1]
     depth = slab_values.shape[0]
-    sent_y, sent_z = len(ring_order(n, [0, 1], True)) * 2, len(ring_order(n, [0, 1], True))
+    sent_y, sent_z = len(panel_order(n, True)), len(ring_order(n, True, 2))
     dma = pltpu.SemaphoreType.DMA
     held = [pltpu.VMEM((TAB + NNZ * BS, BS), jnp.bfloat16) for _ in range(2 * n)]
     half = 2 * BS
     return pl.pallas_call(
         functools.partial(kernel, n),
         out_shape=jax.ShapeDtypeStruct((4 * BS, width), jnp.bfloat16),
-        in_specs=[
-            pl.BlockSpec(memory_space=pl.ANY),
-            pl.BlockSpec(memory_space=pl.ANY),
-            pl.BlockSpec(memory_space=pltpu.SMEM),
-            pl.BlockSpec(memory_space=pltpu.SMEM),
-        ],
+        in_specs=[pl.BlockSpec(memory_space=pl.ANY)] * 4,
         out_specs=pl.BlockSpec(memory_space=pltpu.VMEM),
         scratch_shapes=held
         + [
+            pltpu.SMEM((RB,), jnp.int32),
+            pltpu.SMEM(pattern_result.shape, jnp.int32),
             pltpu.VMEM((RB, BS, BS), jnp.bfloat16),
             pltpu.VMEM((n * depth, width), jnp.bfloat16),
             pltpu.VMEM((RB * BS, n * 2 * BS), jnp.bfloat16),
             pltpu.VMEM((6, half, width), jnp.float32),
             pltpu.VMEM((2, half, width), jnp.float32),
             pltpu.VMEM((4, half, width), jnp.float32),
-            dma((2,)),
+            dma((4,)),
             dma((2 * sent_y,)),
             dma((2 * sent_y,)),
             dma((4 * n,)),
@@ -273,7 +304,7 @@
             dma((6,)),
             dma((6,)),
         ],
-        compiler_params=pltpu.CompilerParams(collective_id=0, has_side_effects=True, vmem_limit_bytes=48 * 1024 * 1024),
+        compiler_params=pltpu.CompilerParams(collective_id=0, has_side_effects=True, vmem_limit_bytes=60 * 1024 * 1024),
         cost_estimate=pl.CostEstimate(flops=2 * RB * BS * n * 2 * BS * width, bytes_accessed=1 << 22, transcendentals=0),
     )(panel_values.reshape(RB, BS, block), slab_values, pattern_panel[:, 0], pattern_result)
 

time: 71.3 us -> 65.7 us (0.921)
  Pallas kernels: 67.2 us -> 63.7 us
  local copies, waits for them, and re-layouts: 3.4 us -> 1.78 us
    pallas_call x1, Pallas kernels: 67.2 us -> 63.7 us  [per_device(): pl.pallas_call(functools.partial(kernel, n), out_shape=jax.ShapeDtypeStru...]
    unnamed x9 -> x1, local copies, waits for them, and re-layouts: 3.4 us -> 1.78 us
where the time goes in v2:
time: 65.7 us; the launch traced here: 65.5 us
  Pallas kernels  63.7 us (97%)
  local copies, waits for them, and re-layouts  1.78 us (3%)
    pallas_call x1, Pallas kernels, per_device(): pl.pallas_call(functools.partial(kernel, n), out_shape=jax.ShapeDtypeStru...  63.7 us
    unnamed x1, local copies, waits for them, and re-layouts  1.78 us

profile of v2, /device:TPU:1, one launch (start us, length us, event | category | flops | bytes accessed | tf_op | source)
XLA Modules:
  0.0 65.5 jit_solution(4578668857581680394)
XLA Ops:
  0.0 63.7 %shard_map.46 = bf16[512,384]{1,0:T(8,128)(2,1)} custom-call(bf16[16,128,128]{2,1,0:T(8,128)(2,1)} %bitcast.2, bf16[256,384]{1,0:T(8,128)(2,1)} %slab_hbm.1, s32[16]{0:T(128)} %bitcast.3, s32[4,3]{1,0:T(4,128)} %keep_hbm.1), custom_call_target="tpu_custom_call" | custom-call | flops 3221225472 | bytes 4194304 | tf_op jit(solution)/shard_map/pallas_call | solution.py:282
  63.7 1.8 %copy.6 = bf16[512,384]{1,0:T(8,128)(2,1)} copy(bf16[512,384]{1,0:T(8,128)(2,1)} %shard_map.46) | data formatting | bytes 786432

commit v3 on v2

--- a/solution.py
+++ b/solution.py
@@ -13,6 +13,8 @@
 TAB = 16
 NL = 4
 UNITS = ((2, 0), (2, 1), (1, 1), (3, 0), (1, 0), (3, 1), (0, 0), (0, 1))
+GROUP = 32
+TOP = 32767.0
 Y_STEP, Z_STEP = 1.7, 2.45
 
 
@@ -42,7 +44,7 @@
 
 def kernel(n, panel_hbm, slab_hbm, flags_hbm, keep_hbm, out, *scratch):
     held = scratch[: 2 * n]
-    (flags, keep, panel, slab, dense, send_x, mid_x, last_x, own_sem, y_send, y_recv, c_send, c_recv, z_send, z_recv, x_send, x_recv) = scratch[2 * n :]
+    (flags, keep, panel, slab, dense, own, send_x, send_s, got_x, got_s, own_sem, y_send, y_recv, c_send, c_recv, z_send, z_recv, x_send, x_recv, s_send, s_recv) = scratch[2 * n :]
     col, z, layer = lax.axis_index("col"), lax.axis_index("row"), lax.axis_index("layer")
     y, core = col // 2, lax.rem(col, 2)
     depth = slab_hbm.shape[0]
@@ -155,17 +157,34 @@
     def multiply(unit):
         return jnp.dot(dense[pl.ds(unit * 2 * BS, 2 * BS), :], slab[...], preferred_element_type=jnp.float32)
 
-    def x_copy(k, device, dst):
-        return remote(send_x.at[k], dst, x_send.at[k], x_recv.at[k], device)
-
-    x_copies = [
-        x_copy(0, x_next[1], mid_x.at[0]),
-        x_copy(1, x_next[-1], mid_x.at[1]),
-        x_copy(2, x_next[1], last_x.at[0]),
-        x_copy(3, x_next[-1], last_x.at[1]),
-        x_copy(4, x_next[1], last_x.at[2]),
-        x_copy(5, x_next[-1], last_x.at[3]),
-    ]
+    def spans(rows=2 * BS):
+        return [(g, slice(g * GROUP, (g + 1) * GROUP)) for g in range(rows // GROUP)]
+
+    def encode(u, total):
+        for g, span in spans():
+            values = total[span]
+            largest = jnp.maximum(jnp.max(jnp.abs(values), axis=0, keepdims=True), 4e-34)
+            send_s[u, g : g + 1, :] = largest * (1.0 / TOP)
+            send_x[u, span, :] = jnp.round(values * (TOP / largest)).astype(jnp.int32).astype(jnp.int16)
+
+    def decode(u, g, span):
+        return got_x[u, span, :].astype(jnp.int32).astype(jnp.float32) * got_s[u, g : g + 1, :]
+
+    def x_copies(u):
+        device = x_next[1 if u % 2 == 0 else -1]
+        return (
+            remote(send_s.at[u], got_s.at[u], s_send.at[u], s_recv.at[u], device),
+            remote(send_x.at[u], got_x.at[u], x_send.at[u], x_recv.at[u], device),
+        )
+
+    def x_begin(u, total):
+        encode(u, total)
+        for copy in x_copies(u):
+            begin(copy)
+
+    def x_wait(u):
+        for copy in x_copies(u):
+            copy.wait_recv()
 
     def follow(copy_of, after, event):
         for i, at in enumerate(after):
@@ -212,8 +231,7 @@
     computed = [0]
 
     def early_unit(u):
-        send_x[u] = multiply(u)
-        begin(x_copies[u])
+        x_begin(u, multiply(u))
 
     z_left = len(z_order[1])
     for _, kind, i in sorted(events):
@@ -245,28 +263,24 @@
         early_unit(u)
     for u in (2, 3):
         early_unit(u)
-    for u, k in ((4, 0), (5, 1)):
-        own = multiply(u)
-        x_copies[k].wait_recv()
-        send_x[u] = own + mid_x[k]
-        begin(x_copies[u])
-    top, low = multiply(6), multiply(7)
-    half = 2 * BS
-
-    def finish(total, first):
-        for r in range(2):
+    for u in (4, 5):
+        total = multiply(u)
+        x_wait(u - 4)
+        x_begin(u, jnp.concatenate([total[span] + decode(u - 4, g, span) for g, span in spans()], axis=0))
+    for i in range(2):
+        own[i] = multiply(6 + i)
+    for i, u in ((0, 3), (1, 2)):
+        x_wait(u)
+        for g, span in spans():
+            own[i, span, :] += decode(u, g, span)
+    for i, u in ((0, 4), (1, 5)):
+        x_wait(u)
+        for g, span in spans():
+            total = own[i, span, :] + decode(u, g, span)
             for c in range(total.shape[1] // BS):
-                kept = keep[first // BS + r, c].astype(jnp.float32)
-                out[pl.ds(first + r * BS, BS), pl.ds(c * BS, BS)] = (total[r * BS : (r + 1) * BS, c * BS : (c + 1) * BS] * kept).astype(jnp.bfloat16)
-
-    x_copies[3].wait_recv()
-    send_top = top + last_x[1]
-    x_copies[2].wait_recv()
-    send_low = low + last_x[0]
-    x_copies[4].wait_recv()
-    finish(send_top + last_x[2], 0)
-    x_copies[5].wait_recv()
-    finish(send_low + last_x[3], half)
+                kept = keep[2 * i + g * GROUP // BS, c].astype(jnp.float32)
+                at = slice(c * BS, (c + 1) * BS)
+                out[pl.ds(2 * i * BS + g * GROUP, GROUP), at] = (total[:, at] * kept).astype(jnp.bfloat16)
     for copy in started:
         copy.wait_send()
 
@@ -291,9 +305,11 @@
             pltpu.VMEM((RB, BS, BS), jnp.bfloat16),
             pltpu.VMEM((n * depth, width), jnp.bfloat16),
             pltpu.VMEM((RB * BS, n * 2 * BS), jnp.bfloat16),
-            pltpu.VMEM((6, half, width), jnp.float32),
             pltpu.VMEM((2, half, width), jnp.float32),
-            pltpu.VMEM((4, half, width), jnp.float32),
+            pltpu.VMEM((6, half, width), jnp.int16),
+            pltpu.VMEM((6, half // GROUP, width), jnp.float32),
+            pltpu.VMEM((6, half, width), jnp.int16),
+            pltpu.VMEM((6, half // GROUP, width), jnp.float32),
             dma((4,)),
             dma((2 * sent_y,)),
             dma((2 * sent_y,)),
@@ -301,6 +317,8 @@
             dma((4 * n,)),
             dma((2 * sent_z,)),
             dma((2 * sent_z,)),
+            dma((6,)),
+            dma((6,)),
             dma((6,)),
             dma((6,)),
         ],

time: 65.7 us -> 57.2 us (0.87)
  Pallas kernels: 63.7 us -> 55.2 us
    pallas_call x1, Pallas kernels: 63.7 us -> 55.2 us  [per_device(): pl.pallas_call(functools.partial(kernel, n), out_shape=jax.ShapeDtypeStru...]
where the time goes in v3:
time: 57.2 us; the launch traced here: 57 us
  Pallas kernels  55.2 us (97%)
  local copies, waits for them, and re-layouts  1.78 us (3%)
    pallas_call x1, Pallas kernels, per_device(): pl.pallas_call(functools.partial(kernel, n), out_shape=jax.ShapeDtypeStru...  55.2 us
    unnamed x1, local copies, waits for them, and re-layouts  1.78 us

profile of v3, /device:TPU:1, one launch (start us, length us, event | category | flops | bytes accessed | tf_op | source)
XLA Modules:
  0.0 57.0 jit_solution(16047872214748772795)
XLA Ops:
  0.0 55.2 %shard_map.46 = bf16[512,384]{1,0:T(8,128)(2,1)} custom-call(bf16[16,128,128]{2,1,0:T(8,128)(2,1)} %bitcast.2, bf16[256,384]{1,0:T(8,128)(2,1)} %slab_hbm.1, s32[16]{0:T(128)} %bitcast.3, s32[4,3]{1,0:T(4,128)} %keep_hbm.1), custom_call_target="tpu_custom_call" | custom-call | flops 3221225472 | bytes 4194304 | tf_op jit(solution)/shard_map/pallas_call | solution.py:296
  55.2 1.8 %copy.6 = bf16[512,384]{1,0:T(8,128)(2,1)} copy(bf16[512,384]{1,0:T(8,128)(2,1)} %shard_map.46) | data formatting | bytes 786432

commit v4 on v3

v4 whole, which is shorter than its diff:
```python
import functools

import jax
import jax.numpy as jnp
from jax import lax
from jax.experimental import pallas as pl
from jax.experimental.pallas import tpu as pltpu
from jax.sharding import PartitionSpec as P

BS = 128
RB = 16
NNZ = 8
TAB = 16
NL = 4
UNITS = [((to, 0, r), (to, 1, r)) if to in (0, 2) else ((1, 1 - e, r), (3, e, r)) for to, e in ((2, 0), (1, 0), (1, 1), (0, 0)) for r in (0, 1)]
GROUP = 32
TOP = 32767.0
PIECES = ((0, 2), (2, 2), (4, 2), (6, 2))
SLOT_US, HOP_US, Z_US, Z_LATE = 0.76, 2.7, 2.37, 2.0
WINDOW = 8


def ring_order(n, forward, pieces):
    own = list(range(pieces)) if forward else list(range(pieces))[::-1]
    return [(step, q) for step in range(n // 2) for q in (own if step < n // 2 - 1 else own[: pieces // 2])]


def panel_order(n, forward):
    a, b, c, d = range(len(PIECES)) if forward else (1, 0, 3, 2)
    plan = [(0, a), (0, b), (0, c), (1, a), (1, b), (0, d), (2, a), (2, b), (1, c), (1, d), (3, a), (2, c), (2, d), (3, c)]
    last = n // 2 - 1
    order, ready, now = [], {}, 0.0
    for step, q in plan:
        if step < last or step == last and q in (a, c):
            now = max(now, ready.get(q, 0.0)) + PIECES[q][1] * SLOT_US
            ready[q] = now + HOP_US
            order.append(((step, q), ready[q]))
    return order


def triggers(order, depth, size):
    after = []
    for m, (step, q) in enumerate(order):
        needs = order.index((step - 1, q)) if step else -1
        room = next(e for e in range(-1, m) if sum(size(r) for _, r in order[e + 1 : m + 1]) <= depth)
        after.append(max(after[-1] if after else -1, needs, room))
    return after


def kernel(n, panel_hbm, slab_hbm, flags_hbm, keep_hbm, out, *scratch):
    held = scratch[: 2 * n]
    (flags, keep, panel, slab, dense, own, send_x, send_s, got_x, got_s, own_sem, y_send, y_recv, c_send, c_recv, z_send, z_recv, x_send, x_recv, s_send, s_recv) = scratch[2 * n :]
    col, z, layer = lax.axis_index("col"), lax.axis_index("row"), lax.axis_index("layer")
    y, core = col // 2, lax.rem(col, 2)
    depth = slab_hbm.shape[0]
    part = depth // 2

    def beside(place, count, step):
        return lax.rem(place + step + count, count)

    y_next = {+1: {"col": beside(y, n, 1) * 2 + core}, -1: {"col": beside(y, n, -1) * 2 + core}}
    z_next = {+1: {"row": beside(z, n, 1)}, -1: {"row": beside(z, n, -1)}}
    x_next = {+1: {"layer": beside(layer, NL, 1)}, -1: {"layer": beside(layer, NL, -1)}}
    sibling = {"col": y * 2 + 1 - core}
    neighbours = [y_next[1], y_next[-1], z_next[1], z_next[-1], x_next[1], x_next[-1], sibling]
    barrier = pltpu.get_barrier_semaphore()
    for device in neighbours:
        pl.semaphore_signal(barrier, inc=1, device_id=device, device_id_type=pl.DeviceIdType.MESH)

    flags_in = pltpu.make_async_copy(flags_hbm, flags, own_sem.at[0])
    flags_in.start()
    panel_in = pltpu.make_async_copy(panel_hbm, panel, own_sem.at[1])
    panel_in.start()
    slab_in = pltpu.make_async_copy(slab_hbm, slab.at[pl.ds(pl.multiple_of(z * depth, depth), depth)], own_sem.at[2])
    slab_in.start()
    keep_in = pltpu.make_async_copy(keep_hbm, keep, own_sem.at[3])
    keep_in.start()

    rows_of = []
    for ahead, half, r in sum(UNITS, ()):
        rows_of.append(lax.rem(layer + ahead, NL) * (RB // NL) + half * 2 + r)
    count = jnp.int32(0)
    source = [jnp.int32(0)] * NNZ
    table = jnp.full((TAB, BS), float(NNZ), jnp.float32)
    place_of = lax.broadcasted_iota(jnp.int32, (TAB, BS), 0)
    flags_in.wait()
    for p in range(RB):
        flag = flags[rows_of[p]]
        if p > RB - NNZ:
            count = jnp.maximum(count, p - (RB - NNZ))
        for s in range(max(0, p - (RB - NNZ)), min(p, NNZ - 1) + 1):
            source[s] = jnp.where((flag == 1) & (count == s), rows_of[p], source[s])
        slot = jnp.where(flag == 1, count, NNZ)
        table = jnp.where(place_of == p, slot.astype(jnp.float32), table)
        count = count + flag
    held[0][pl.ds(0, TAB), :] = table.astype(jnp.bfloat16)
    panel_in.wait()

    def pack(q):
        for s in range(PIECES[q][0], sum(PIECES[q])):
            held[0][pl.ds(TAB + s * BS, BS), :] = panel[source[s]]

    pack(0)
    pack(1)
    slab_in.wait()
    keep_in.wait()
    pl.semaphore_wait(barrier, len(neighbours))

    started = []

    def remote(src, dst, send, recv, device):
        return pltpu.make_async_remote_copy(src_ref=src, dst_ref=dst, send_sem=send, recv_sem=recv, device_id=device, device_id_type=pl.DeviceIdType.MESH)

    def begin(copy):
        copy.start()
        started.append(copy)

    def rows(q):
        slot, slots = PIECES[q]
        return pl.ds(0, TAB + slots * BS) if slot == 0 else pl.ds(TAB + slot * BS, slots * BS)

    y_order = {d: [item for item, _ in panel_order(n, d == 1)] for d in (1, -1)}
    z_order = {d: ring_order(n, d == 1, 2) for d in (1, -1)}
    y_after, z_after = triggers(y_order[1], WINDOW, lambda q: PIECES[q][1]), triggers(z_order[1], 2, lambda q: 1)

    def y_copy(d, i):
        step, q = y_order[d][i]
        src, dst = held[2 * ((-d * step) % n)], held[2 * ((-d * (step + 1)) % n)]
        k = (0 if d == 1 else len(y_order[1])) + i
        return remote(src.at[rows(q)], dst.at[rows(q)], y_send.at[k], y_recv.at[k], y_next[d])

    def c_copy(j, q):
        return remote(held[2 * j].at[rows(q)], held[2 * j + 1].at[rows(q)], c_send.at[len(PIECES) * j + q], c_recv.at[len(PIECES) * j + q], sibling)

    def z_copy(d, i, back=0):
        step, q = z_order[d][i]
        k = (0 if d == 1 else len(z_order[1])) + i
        at = slab.at[pl.ds(pl.multiple_of(beside(z, n, -d * (step + back)) * depth + q * part, part), part)]
        return remote(at, at, z_send.at[k], z_recv.at[k], z_next[d])

    def lanes(j, c):
        side = core if c == 0 else 1 - core
        return pl.ds(pl.multiple_of(beside(y, n, j) * 2 * BS + side * BS, BS), BS)

    def unpack(j, c, places):
        ref, where = held[2 * j + c], lanes(j, c)
        slots = range(min(NNZ, places[-1] + 1))
        one_of = {}
        for p in places:
            line = ref[pl.ds(0, TAB), :][p : p + 1, :].astype(jnp.float32)
            for s in slots:
                if p - (RB - NNZ) <= s <= p:
                    one_of[p, s] = (line == float(s)).astype(jnp.bfloat16)

        @pl.loop(0, BS // 16)
        def _(i):
            values = [ref[pl.ds(pl.multiple_of(TAB + s * BS + i * 16, 16), 16), :] for s in slots]
            for p in places:
                terms = [values[s] * one_of[p, s] for s in slots if (p, s) in one_of]
                dense[pl.ds(pl.multiple_of(p * BS + i * 16, 16), 16), where] = functools.reduce(jnp.add, terms)

    def multiply(unit):
        return jnp.dot(dense[pl.ds(unit * 2 * BS, 2 * BS), :], slab[...], preferred_element_type=jnp.float32)

    spans = [(g, slice(g * GROUP, (g + 1) * GROUP)) for g in range(BS // GROUP)]

    def encode(k, total):
        for g, span in spans:
            values = total[span]
            largest = jnp.maximum(jnp.max(jnp.abs(values), axis=0, keepdims=True), 4e-34)
            send_s[k, g : g + 1, :] = largest * (1.0 / TOP)
            send_x[k, span, :] = jnp.round(values * (TOP / largest)).astype(jnp.int32).astype(jnp.int16)

    def decode(k, g, span):
        return got_x[k, span, :].astype(jnp.int32).astype(jnp.float32) * got_s[k, g : g + 1, :]

    def x_copies(k):
        device = x_next[1 if k % 2 == 0 else -1]
        return (
            remote(send_s.at[k], got_s.at[k], s_send.at[k], s_recv.at[k], device),
            remote(send_x.at[k], got_x.at[k], x_send.at[k], x_recv.at[k], device),
        )

    def x_begin(k, total):
        encode(k, total)
        for copy in x_copies(k):
            begin(copy)

    def x_wait(k):
        for copy in x_copies(k):
            copy.wait_recv()

    def follow(copy_of, after, event, sides=(1, -1)):
        for i, at in enumerate(after):
            if at == event:
                for d in sides:
                    begin(copy_of(d, i))

    first = [(d, i) for i, at in enumerate(y_after) if at == -1 for d in (1, -1)]
    packed = {0, 1}
    for d, i in first:
        if y_order[d][i][1] in packed:
            begin(y_copy(d, i))
    follow(z_copy, z_after, -1)
    for q in range(2, len(PIECES)):
        pack(q)
    for d, i in first:
        if y_order[d][i][1] not in packed:
            begin(y_copy(d, i))
    everything = set(range(len(PIECES)))
    for q in range(len(PIECES)):
        begin(c_copy(0, q))

    arrived, passed = {0: set(everything)}, {0: set(everything)}
    tiers = (((0, 1), range(4)), ((0, 1, 2), range(4, 6)), (range(len(PIECES)), range(6, RB)))
    done = set()
    waited = set()

    def drain(c, source_of):
        for j in range(n):
            for tier, (pieces, places) in enumerate(tiers):
                if (j, c, tier) in done or not set(pieces) <= source_of.get(j, set()):
                    continue
                for q in pieces if c == 1 else ():
                    if (j, q) not in waited:
                        waited.add((j, q))
                        c_copy(j, q).wait_recv()
                done.add((j, c, tier))
                unpack(j, c, places)

    events = [(us, 0, i) for i, (_, us) in enumerate(panel_order(n, True))]
    events += [(Z_US * (i + 1) + HOP_US + Z_LATE, 1, i) for i in range(len(z_order[1]))]
    computed = [0]

    def early_unit(u):
        total = multiply(u)
        for side in range(2):
            x_begin(2 * u + side, total[side * BS : (side + 1) * BS])

    z_left = len(z_order[1])
    for _, kind, i in sorted(events):
        if kind == 1:
            for d in (1, -1):
                z_copy(d, i, 1).wait_recv()
                follow(z_copy, z_after, i, (d,))
            z_left -= 1
            continue
        landed = []
        before = {j: set(v) for j, v in passed.items()}
        for d in (1, -1):
            step, q = y_order[d][i]
            j = (-d * (step + 1)) % n
            y_copy(d, i).wait_recv()
            follow(y_copy, y_after, i, (d,))
            landed.append((j, q))
            arrived.setdefault(j, set()).add(q)
            passed.setdefault(j, set()).add(q)
        for j, q in landed:
            begin(c_copy(j, q))
        for turn in range(2):
            u = computed[0]
            if turn == 0 and i >= max(y_after) or turn == 1 and i < max(y_after):
                if z_left == 0 and u < 2 and all((j, c, 0) in done for j in range(n) for c in range(2)):
                    early_unit(u)
                    computed[0] += 1
            if turn == 0 and i < len(y_order[1]) - 1:
                drain(0, arrived)
                drain(1, before)
    drain(0, arrived)
    drain(1, passed)
    for u in range(computed[0], 4):
        early_unit(u)
    for u in (4, 5):
        total = multiply(u)
        for side in range(2):
            k = 2 * (u - 4) + side
            x_wait(k)
            x_begin(2 * u + side, jnp.concatenate([total[side * BS :][span] + decode(k, g, span) for g, span in spans], axis=0))
    for r in range(2):
        total = multiply(6 + r)
        for half in range(2):
            own[half * 2 + r] = total[half * BS : (half + 1) * BS]
    for r in range(2):
        for half in range(2):
            k = 2 * (2 + r) + 1 - half
            x_wait(k)
            for g, span in spans:
                own[half * 2 + r, span, :] += decode(k, g, span)
    for r in range(2):
        for half in range(2):
            k = 2 * (4 + r) + half
            x_wait(k)
            for g, span in spans:
                total = own[half * 2 + r, span, :] + decode(k, g, span)
                for c in range(total.shape[1] // BS):
                    kept = keep[half * 2 + r, c].astype(jnp.float32)
                    at = slice(c * BS, (c + 1) * BS)
                    out[pl.ds((half * 2 + r) * BS + g * GROUP, GROUP), at] = (total[:, at] * kept).astype(jnp.bfloat16)
    for copy in started:
        copy.wait_send()


def per_device(n, panel_values, slab_values, pattern_panel, pattern_result):
    block = panel_values.shape[1]
    width = slab_values.shape[1]
    depth = slab_values.shape[0]
    sent_y, sent_z = len(panel_order(n, True)), len(ring_order(n, True, 2))
    dma = pltpu.SemaphoreType.DMA
    held = [pltpu.VMEM((TAB + NNZ * BS, BS), jnp.bfloat16) for _ in range(2 * n)]
    return pl.pallas_call(
        functools.partial(kernel, n),
        out_shape=jax.ShapeDtypeStruct((4 * BS, width), jnp.bfloat16),
        in_specs=[pl.BlockSpec(memory_space=pl.ANY)] * 4,
        out_specs=pl.BlockSpec(memory_space=pltpu.VMEM),
        scratch_shapes=held
        + [
            pltpu.SMEM((RB,), jnp.int32),
            pltpu.SMEM(pattern_result.shape, jnp.int32),
            pltpu.VMEM((RB, BS, BS), jnp.bfloat16),
            pltpu.VMEM((n * depth, width), jnp.bfloat16),
            pltpu.VMEM((RB * BS, n * 2 * BS), jnp.bfloat16),
            pltpu.VMEM((4, BS, width), jnp.float32),
            pltpu.VMEM((12, BS, width), jnp.int16),
            pltpu.VMEM((12, BS // GROUP, width), jnp.float32),
            pltpu.VMEM((12, BS, width), jnp.int16),
            pltpu.VMEM((12, BS // GROUP, width), jnp.float32),
            dma((4,)),
            dma((2 * sent_y,)),
            dma((2 * sent_y,)),
            dma((len(PIECES) * n,)),
            dma((len(PIECES) * n,)),
            dma((2 * sent_z,)),
            dma((2 * sent_z,)),
            dma((12,)),
            dma((12,)),
            dma((12,)),
            dma((12,)),
        ],
        compiler_params=pltpu.CompilerParams(collective_id=0, has_side_effects=True, vmem_limit_bytes=60 * 1024 * 1024),
        cost_estimate=pl.CostEstimate(flops=2 * RB * BS * n * 2 * BS * width, bytes_accessed=1 << 22, transcendentals=0),
    )(panel_values.reshape(RB, BS, block), slab_values, pattern_panel[:, 0], pattern_result)


def solution(mesh):
    placed = (
        P("row", ("layer", "col")),
        P(("layer", "row"), "col"),
        P("row", ("layer", "col")),
        P(("row", "layer"), "col"),
    )
    return jax.shard_map(
        functools.partial(per_device, mesh.shape["row"]),
        mesh=mesh,
        in_specs=placed,
        out_specs=P(("row", "layer"), "col"),
        check_vma=False,
    )
```

time: 57.2 us -> 55.9 us (0.977)
  Pallas kernels: 55.2 us -> 53.9 us
    pallas_call x1, Pallas kernels: 55.2 us -> 53.9 us  [per_device(): pl.pallas_call(functools.partial(kernel, n), out_shape=jax.ShapeDtypeStru...]
where the time goes in v4:
time: 55.9 us; the launch traced here: 55.7 us
  Pallas kernels  53.9 us (96%)
  local copies, waits for them, and re-layouts  1.78 us (3%)
    pallas_call x1, Pallas kernels, per_device(): pl.pallas_call(functools.partial(kernel, n), out_shape=jax.ShapeDtypeStru...  53.9 us
    unnamed x1, local copies, waits for them, and re-layouts  1.78 us

profile of v4, /device:TPU:1, one launch (start us, length us, event | category | flops | bytes accessed | tf_op | source)
XLA Modules:
  0.0 55.7 jit_solution(3563823944999563123)
XLA Ops:
  0.0 53.9 %shard_map.46 = bf16[512,384]{1,0:T(8,128)(2,1)} custom-call(bf16[16,128,128]{2,1,0:T(8,128)(2,1)} %bitcast.2, bf16[256,384]{1,0:T(8,128)(2,1)} %slab_hbm.1, s32[16]{0:T(128)} %bitcast.3, s32[4,3]{1,0:T(4,128)} %keep_hbm.1), custom_call_target="tpu_custom_call" | custom-call | flops 3221225472 | bytes 4194304 | tf_op jit(solution)/shard_map/pallas_call | solution.py:310
  53.9 1.8 %copy.6 = bf16[512,384]{1,0:T(8,128)(2,1)} copy(bf16[512,384]{1,0:T(8,128)(2,1)} %shard_map.46) | data formatting | bytes 786432
